TPU v7x, 32 devices: a whole 2x2x4 slice. The times are simulated.
32 devices in a mesh: seq: 16 (over z, y, core), kv: 2 (over x).
Axes of the slice: x: 2, y: 2, z: 4, core: 2. Of those that a mesh axis runs over, the one named last changes fastest.
Arguments:
- plan: int32 [16], replicated, may hold values from 0 to 15, each once
- queries: bfloat16 [2048, 1024], P('seq', 'kv'), may hold values from -24 to 24
- keys: bfloat16 [2048, 256], P('seq', 'kv'), may hold values from -9 to 9
- student_c: bfloat16 [2048, 1024], P('seq', 'kv'), may hold values from -0.125 to 0.125
- layer_input: bfloat16 [2048, 8192], P('seq', 'kv'), may hold values from -6 to 6
- b_weight: bfloat16 [2, 8192, 128], P('kv'), may hold values from -0.0625 to 0.0625
Outputs:
- grad_c: bfloat16 [2048, 1024], P('seq', 'kv')
- grad_wb: float32 [2, 8192, 128], P('kv', 'seq')
Inputs may be any that keep to these rules, and one draw needn't show every extreme that they name: Each value appears once: plan[d] is the block of 128 consecutive positions held by index d of seq.
All inputs are finite; a program needn't handle non-finite values.
Results may differ from a plain program's by a relative error of at most 0.0049.
Values may be sent and summed in bfloat16 or wider, within the bound.
A program may use at most 64 MiB of HBM per device.

v0:
```python
import math
import jax
import jax.numpy as jnp
from jax import lax
from jax.sharding import PartitionSpec as P

NEG_FILL = -1e30


def block_sweep(update, running, pieces, shard_rows):
    total_rows = pieces[0].shape[0]
    shard_count = total_rows // shard_rows
    block_limit = max(1, 1024 // shard_rows)
    factor = 1
    for option in range(1, shard_count + 1):
        if shard_count % option == 0 and option <= block_limit:
            factor = option
    block_rows = factor * shard_rows
    block_count = total_rows // block_rows
    stacked = tuple(
        (member.reshape((block_count, block_rows) + member.shape[1:]) for member in pieces)
    )
    offsets = block_rows * jnp.arange(block_count, dtype=jnp.int32)

    def advance(partial_state, inputs):
        return (update(partial_state, inputs[0], inputs[1]), None)

    running, unused = lax.scan(advance, running, (stacked, offsets))
    return running


def local(plan, queries, keys, student_c, layer_input, b_weight):
    shard_rows = keys.shape[0]
    state_width = keys.shape[1]
    head_count = queries.shape[1] // state_width
    seq_count = lax.axis_size("seq")
    token_count = shard_rows * seq_count
    student_scale = 2.0 / math.sqrt(token_count)
    score_scale = 1.0 / math.sqrt(state_width)
    block_ids = jnp.arange(seq_count, dtype=jnp.int32)

    def positions_of(global_rows):
        owner_ids = global_rows // shard_rows
        picked = jnp.sum(
            jnp.where(owner_ids[:, None] == block_ids[None, :], plan[None, :], 0), axis=1
        )
        return picked * shard_rows + global_rows % shard_rows

    own_start = lax.axis_index("seq") * shard_rows
    query_pos = positions_of(own_start + jnp.arange(shard_rows, dtype=jnp.int32))
    query_heads = queries.reshape(shard_rows, head_count, state_width)
    student_heads = student_c.reshape(shard_rows, head_count, state_width)
    features = lax.all_gather(layer_input, "kv", axis=1, tiled=True)
    b_local = jnp.dot(features, b_weight[0], preferred_element_type=jnp.float32).astype(
        jnp.bfloat16
    )

    def scores_of(key_block, offset):
        key_pos = positions_of(offset + jnp.arange(key_block.shape[0], dtype=jnp.int32))
        visible = key_pos[None, None, :] <= query_pos[:, None, None]
        scores = (
            jnp.einsum("qhd,kd->qhk", query_heads, key_block, preferred_element_type=jnp.float32)
            * score_scale
        )
        return (jnp.where(visible, scores, NEG_FILL), visible)

    def stats_step(running, members, offset):
        highest, totals = running
        scores, visible = scores_of(members[0], offset)
        raised = jnp.maximum(highest, jnp.max(scores, axis=-1))
        weights = jnp.where(visible, jnp.exp(scores - raised[..., None]), 0.0)
        return (raised, totals * jnp.exp(highest - raised) + jnp.sum(weights, axis=-1))

    def pair_step(highest, totals):

        def advance_pair(running, members, offset):
            grad_acc, db_buffer = running
            key_block, b_block = members
            scores, visible = scores_of(key_block, offset)
            teacher = jnp.where(
                visible, jnp.exp(scores - highest[..., None]) / totals[..., None], 0.0
            )
            student = student_scale * jnp.einsum(
                "qhd,kd->qhk", student_heads, b_block, preferred_element_type=jnp.float32
            )
            residual = jnp.where(visible, student - teacher, 0.0).astype(jnp.bfloat16)
            grad_acc = grad_acc + jnp.einsum(
                "qhk,kd->qhd", residual, b_block, preferred_element_type=jnp.float32
            )
            contrib = jnp.einsum(
                "qhk,qhd->kd", residual, student_heads, preferred_element_type=jnp.float32
            )
            db_buffer = lax.dynamic_update_slice_in_dim(db_buffer, contrib, offset, 0)
            return (grad_acc, db_buffer)

        return advance_pair

    stats_init = (
        jnp.full((shard_rows, head_count), NEG_FILL, jnp.float32),
        jnp.zeros((shard_rows, head_count), jnp.float32),
    )
    pair_init = (
        jnp.zeros((shard_rows, head_count, state_width), jnp.float32),
        jnp.zeros((token_count, state_width), jnp.float32),
    )
    highest, totals = block_sweep(
        stats_step, stats_init, (lax.all_gather(keys, "seq", axis=0, tiled=True),), shard_rows
    )
    advance_pair = pair_step(highest, totals)
    grad_acc, db_buffer = block_sweep(
        advance_pair,
        pair_init,
        (
            lax.all_gather(keys, "seq", axis=0, tiled=True),
            lax.all_gather(b_local, "seq", axis=0, tiled=True),
        ),
        shard_rows,
    )
    arrived = lax.all_to_all(
        db_buffer.reshape(seq_count, shard_rows, state_width).astype(jnp.bfloat16),
        "seq",
        split_axis=0,
        concat_axis=0,
        tiled=True,
    ).astype(jnp.float32)
    b_grad = jnp.sum(arrived, axis=0).astype(jnp.bfloat16)
    weight_grad = lax.psum_scatter(
        jnp.einsum("td,tn->dn", features, b_grad, preferred_element_type=jnp.float32),
        "seq",
        scatter_dimension=0,
        tiled=True,
    )
    grad_c = grad_acc.reshape(shard_rows, head_count * state_width).astype(jnp.bfloat16)
    return (grad_c, weight_grad[None])


def solution(mesh):
    in_specs = (
        P(),
        P("seq", "kv"),
        P("seq", "kv"),
        P("seq", "kv"),
        P("seq", "kv"),
        P("kv", None, None),
    )
    out_specs = (P("seq", "kv"), P("kv", "seq", None))
    return jax.shard_map(local, mesh=mesh, in_specs=in_specs, out_specs=out_specs, check_vma=False)
```

profile of v0, /device:TPU:0, one launch (start us, length us, event | category | flops | bytes accessed | tf_op | source)
XLA Modules:
  0.0 205.9 jit_solution(17083190945803974519)
XLA Ops:
  7.2 0.7 all-gather.2.cloned.1.call-update
  8.0 0.5 iota_multiply_fusion
  8.5 0.7 select_reduce_fusion.3
  9.3 26.4 %all_gather.12 = bf16[2048,128]{1,0:T(8,128)(2,1)} all-gather(bf16[128,128]{1,0:T(8,128)(2,1)} %param.12), channel_id=1, replica_groups=mesh['seq'=16,'kv'=2] {'seq'}, dimensions={0}, use_global_device_ids=true | all-gather | bytes 557056 | tf_op jit(solution)/shard_map/all_gather | solution.py:114
  35.6 1.0 copy.21
  36.7 0.8 copy.24
  37.6 0.1 copy.23
  37.7 15.4 %while.30 = (s32[]{:T(128)}, f32[128,4]{0,1:T(4,128)S(1)}, f32[128,4]{0,1:T(4,128)S(1)}, s32[2]{0:T(128)}, s32[16]{0:T(128)S(1)}, /*index=5*/s32[128]{0:T(128)S(...) while((s32[]{:T(128)}, f32[128,4]{0,1:T(4,128)S(1)}, ...), condition=%wide.region_5.6_spmd.clone, body=%wide.region_1.5_spmd.clone.sunk | while | flops 138624512 | bytes 5033156 | solution.py:28
  37.7 1.2 dynamic_slice.62
  38.9 0.6 add_select_fusion.6
  39.7 0.6 fusion.70
  40.3 0.2 broadcast_compare_fusion.4
  40.5 2.8 %fusion.71 = (f32[128,4]{0,1:T(4,128)S(1)}, f32[1024,128,4]{1,0,2:T(8,128)}) fusion(pred[128,1024]{0,1:T(8,128)(4,1)S(1)} %broadcast_compare_fusion.4, bf16[128,4,128]{2,0,1:T(8,128)(2,1)} %get-tuple-element.599, bf16[2,1024,128]{2,1,0:T(8,128)(2,1)} %get-tuple-element.598, s32[]{:T(128)} %get-tuple-element.582), kind=kOutput, calls=%fused_computation.4.clone.1 | convolution fusion | flops 135790080 | bytes 2624000 | tf_op jit(solution)/shard_map/while/body/eval_jaxpr/qhd,kd->qhk/dot_general | solution.py:62
  43.3 2.1 %select_reduce_fusion.8 = f32[128,4]{0,1:T(4,128)S(1)} fusion(f32[1024,128,4]{1,0,2:T(8,128)} %get-tuple-element.559, f32[128,4]{0,1:T(4,128)S(1)} %select_maximum_fusion.2, pred[128,1024]{0,1:T(8,128)(4,1)S(1)} %broadcast_compare_fusion.4), kind=kLoop, calls=%fused_computation.3.clone.1 | loop fusion | flops 2620928 | bytes 2232320 | tf_op jit(solution)/shard_map/while/body/eval_jaxpr/reduce_sum | solution.py:72
  45.4 1.2 dynamic_slice.62
  46.6 0.6 add_select_fusion.6
  47.3 0.6 fusion.70
  48.0 0.2 broadcast_compare_fusion.4
  48.2 2.8 %fusion.71 = (f32[128,4]{0,1:T(4,128)S(1)}, f32[1024,128,4]{1,0,2:T(8,128)}) fusion(pred[128,1024]{0,1:T(8,128)(4,1)S(1)} %broadcast_compare_fusion.4, bf16[128,4,128]{2,0,1:T(8,128)(2,1)} %get-tuple-element.599, bf16[2,1024,128]{2,1,0:T(8,128)(2,1)} %get-tuple-element.598, s32[]{:T(128)} %get-tuple-element.582), kind=kOutput, calls=%fused_computation.4.clone.1 | convolution fusion | flops 135790080 | bytes 2624000 | tf_op jit(solution)/shard_map/while/body/eval_jaxpr/qhd,kd->qhk/dot_general | solution.py:62
  51.0 2.1 %select_reduce_fusion.8 = f32[128,4]{0,1:T(4,128)S(1)} fusion(f32[1024,128,4]{1,0,2:T(8,128)} %get-tuple-element.559, f32[128,4]{0,1:T(4,128)S(1)} %select_maximum_fusion.2, pred[128,1024]{0,1:T(8,128)(4,1)S(1)} %broadcast_compare_fusion.4), kind=kLoop, calls=%fused_computation.3.clone.1 | loop fusion | flops 2620928 | bytes 2232320 | tf_op jit(solution)/shard_map/while/body/eval_jaxpr/reduce_sum | solution.py:72
  53.2 2.3 %fusion.41 = bf16[128,128]{1,0:T(8,128)(2,1)S(1)} fusion(bf16[128,8192]{1,0:T(8,128)(2,1)} %all-gather.2.cloned.1.call-done, bf16[1,8192,128]{2,1,0:T(8,128)(2,1)S(1)} %copy-done), kind=kOutput, calls=%fused_computation.67 | convolution fusion | flops 268451840 | bytes 4227072 | tf_op jit(solution)/shard_map/dot_general | solution.py:54
  55.5 20.3 %all_gather.11 = bf16[2048,128]{1,0:T(8,128)(2,1)} all-gather(bf16[128,128]{1,0:T(8,128)(2,1)S(1)} %fusion.41), channel_id=1, replica_groups=mesh['seq'=16,'kv'=2] {'seq'}, dimensions={0}, use_global_device_ids=true | all-gather | bytes 557056 | tf_op jit(solution)/shard_map/all_gather | solution.py:115
  75.7 0.9 broadcast_in_dim.132
  76.6 26.1 %while.31 = (s32[]{:T(128)}, f32[128,4,128]{2,0,1:T(8,128)}, bf16[2048,128]{1,0:T(8,128)(2,1)}, s32[2]{0:T(128)}, s32[16]{0:T(128)S(1)}, /*index=5*/s32[128]{0:T...) while((s32[]{:T(128)}, f32[128,4,128]{2,0,1:T(8,128)}, ...), condition=%wide.region_8.9_spmd.clone, body=%wide.region_6.8_spmd.clone.sunk | while | flops 541930496 | bytes 10123537 | solution.py:28
  76.6 1.3 dynamic_slice.66
  77.8 0.6 add_select_fusion.7
  78.6 0.6 fusion.82
  79.2 0.2 broadcast_compare_fusion.5
  79.4 1.4 fusion.81
  80.8 2.0 fusion.83
  82.8 0.4 convolution_bitcast_fusion.3
  85.2 2.7 %dynamic_update_slice.8 = bf16[2048,128]{1,0:T(8,128)(2,1)} dynamic-update-slice(bf16[2048,128]{1,0:T(8,128)(2,1)} %get-tuple-element.619, bf16[1024,128]{1,0:T(8,128)(2,1)S(1)} %convolution_bitcast_fusion.3, s32[]{:T(128)S(6)} %select_n.206, s32[]{:T(128)} %constant.191.clone.1..sunk.1) | dynamic-update-slice | bytes 524292 | tf_op jit(solution)/shard_map/while/body/eval_jaxpr/dynamic_update_slice | solution.py:93
  87.9 2.1 %convolution_add_fusion.2 = f32[128,4,128]{2,0,1:T(8,128)} fusion(bf16[128,4,1024]{0,2,1:T(8,128)(2,1)S(1)} %fusion.83, f32[128,4,128]{2,0,1:T(8,128)} %get-tuple-element.618, bf16[2,1024,128]{2,1,0:T(8,128)(2,1)} %get-tuple-element.638, s32[]{:T(128)} %get-tuple-element.617, pred[]{:T(512)S(6)} %compare.39), kind=kOutput, calls=%fused_computation.37.clone.1 | convolution fusion | flops 134348800 | bytes 1835521 | tf_op jit(solution)/shard_map/while/body/eval_jaxpr/qhk,kd->qhd/dot_general | solution.py:87
  90.1 1.3 dynamic_slice.66
  91.3 0.6 add_select_fusion.7
  92.1 0.6 fusion.82
  92.7 0.2 broadcast_compare_fusion.5
  92.9 1.4 fusion.81
  94.3 2.0 fusion.83
  96.3 0.4 convolution_bitcast_fusion.3
  98.7 1.8 dynamic_update_slice.8
  100.5 2.2 %convolution_add_fusion.2 = f32[128,4,128]{2,0,1:T(8,128)} fusion(bf16[128,4,1024]{0,2,1:T(8,128)(2,1)S(1)} %fusion.83, f32[128,4,128]{2,0,1:T(8,128)} %get-tuple-element.618, bf16[2,1024,128]{2,1,0:T(8,128)(2,1)} %get-tuple-element.638, s32[]{:T(128)} %get-tuple-element.617, pred[]{:T(512)S(6)} %compare.39), kind=kOutput, calls=%fused_computation.37.clone.1 | convolution fusion | flops 134348800 | bytes 1835521 | tf_op jit(solution)/shard_map/while/body/eval_jaxpr/qhk,kd->qhd/dot_general | solution.py:87
  102.7 18.0 %all_to_all.5 = bf16[16,128,128]{2,1,0:T(8,128)(2,1)S(1)} all-to-all(bf16[16,128,128]{2,1,0:T(8,128)(2,1)} %bitcast.107), channel_id=1, replica_groups=mesh['seq'=16,'kv'=2] {'seq'}, dimensions={0} | all-to-all | bytes 1048576 | tf_op jit(solution)/shard_map/all_to_all | solution.py:119
  120.8 4.2 %convolution_bitcast_fusion.1 = f32[8192,128]{0,1:T(8,128)} fusion(bf16[128,128]{1,0:T(8,128)(2,1)S(1)} %reduce_sum.58, bf16[128,8192]{1,0:T(8,128)(2,1)} %all-gather.2.cloned.1.call-done), kind=kOutput, calls=%fused_computation.64 | convolution fusion | flops 268435456 | bytes 6324224 | tf_op jit(solution)/shard_map/td,tn->dn/dot_general | solution.py:128
  125.0 0.9 copy-done.1
  126.0 0.7 copy_bitcast_fusion
  126.6 70.7 %reduce-scatter.2.cloned.1.call-done = f32[512,128]{0,1:T(8,128)} async-done(((f32[8192,128]{0,1:T(8,128)}), f32[512,128]{0,1:T(8,128)}) %reduce-scatter.2.cloned.1.call-update) | async-done | bytes 262160 | tf_op jit(solution)/shard_map/reduce_scatter | solution.py:127
  197.3 1.8 copy.26
  (28 shorter events, 0.7 us)
Async XLA Ops:
  7.2 46.0 %copy-start = (bf16[1,8192,128]{2,1,0:T(8,128)(2,1)S(1)}, bf16[1,8192,128]{2,1,0:T(8,128)(2,1)}, u32[]{:S(2)}) copy-start(bf16[1,8192,128]{2,1,0:T(8,128)(2,1)} %param.15) | copy-start | bytes 6291460
  7.2 30.5 %copy-start.3 = (s32[16]{0:T(128)S(1)}, s32[16]{0:T(128)}, u32[]{:S(2)}) copy-start(s32[16]{0:T(128)} %param.10) | copy-start | bytes 196
  7.2 30.3 %copy-start.2 = (bf16[128,512]{1,0:T(8,128)(2,1)S(1)}, bf16[128,512]{1,0:T(8,128)(2,1)}, u32[]{:S(2)}) copy-start(bf16[128,512]{1,0:T(8,128)(2,1)} %param.13) | copy-start | bytes 393220
  7.2 45.9 %all-gather.2.cloned.1.call-start = ((), (), s32[]{:S(2)}) async-start(), calls=%async_computation.2 | async-start | bytes 3145728 | tf_op jit(solution)/shard_map/all_gather | solution.py:53
  7.9 189.4 %reduce-scatter.2.cloned.1.call-start = ((), (), s32[]{:S(2)}) async-start(), calls=%async_computation.3 | async-start | bytes 4456448 | tf_op jit(solution)/shard_map/reduce_scatter | solution.py:127
  125.0 0.9 copy-start.1
Sparse Core Ops, SparseCore 0:
  9.6 35.7 all-gather.1
  125.2 72.1 reduce-scatter.1
where the time goes:
time: 207 us; the launch traced here: 206 us
  waiting for transfers between devices  71.4 us (34%)
  blocking collectives  64.6 us (31%)
  matrix products  24.1 us (12%)
  local copies, waits for them, and re-layouts  15.1 us (7%)
  between operations  14.1 us (7%)
  other arithmetic  12.5 us (6%)
  loops' own time  4.02 us (2%)
    reduce_scatter x1, waiting for transfers between devices, local(): lax.psum_scatter(jnp.einsum('td,tn->dn', features, b_grad, preferred_elem...  70.7 us
    all_gather x1, blocking collectives, local(): lax.all_gather(keys, 'seq', axis=0, tiled=True)  26.4 us
    all_gather x1, blocking collectives, local(): lax.all_gather(b_local, 'seq', axis=0, tiled=True)  20.3 us
    all_to_all x1, blocking collectives, local(): lax.all_to_all(db_buffer.reshape(seq_count, shard_rows, state_width).asty...  18 us
    dot_general x4, matrix products, scores_of(): jnp.einsum('qhd,kd->qhk', query_heads, key_block, preferred_element_type=...  9.57 us
    dynamic_slice x4, local copies, waits for them, and re-layouts, block_sweep(): running, unused = lax.scan(advance, running, (stacked, offsets))  4.89 us
    unnamed x13, local copies, waits for them, and re-layouts  4.78 us
    dynamic_update_slice x2, local copies, waits for them, and re-layouts, advance_pair(): db_buffer = lax.dynamic_update_slice_in_dim(db_buffer, contrib, offset, 0)  4.53 us
  transfers between devices with their start and end apart: 2, of which 1 were waited for; matrix products, arithmetic and copies ran while one was open for 9% of the time, Pallas kernels for 0%

commit v1 on v0

--- a/solution.py
+++ b/solution.py
@@ -107,13 +107,38 @@
         stats_step, stats_init, (lax.all_gather(keys, "seq", axis=0, tiled=True),), shard_rows
     )
     advance_pair = pair_step(highest, totals)
+
+    def mix_sizes(array_here, chip_axis, which_dim):
+        earlier, f_now, w_next = (
+            lax.axis_size(chip_axis),
+            lax.axis_index(chip_axis),
+            array_here.shape[which_dim],
+        )
+        frames = [(w, (w + 1) % earlier) for w in range(earlier)]
+        r_now = jnp.zeros(
+            (*array_here.shape[:which_dim], earlier * w_next, *array_here.shape[which_dim + 1 :]),
+            array_here.dtype,
+        )
+        column = [(w, (w - 1) % earlier) for w in range(earlier)]
+        clean = x_next = array_here
+        r_now = lax.dynamic_update_slice_in_dim(r_now, array_here, f_now * w_next, axis=which_dim)
+        back = earlier // 2
+        for j in tuple(range(1, back + 1)):
+            clean = lax.ppermute(clean, chip_axis, frames)
+            r_now = lax.dynamic_update_slice_in_dim(
+                r_now, clean, (f_now - j) % earlier * w_next, axis=which_dim
+            )
+            if j < earlier - back:
+                x_next = lax.ppermute(x_next, chip_axis, column)
+                r_now = lax.dynamic_update_slice_in_dim(
+                    r_now, x_next, (f_now + j) % earlier * w_next, axis=which_dim
+                )
+        return r_now
+
     grad_acc, db_buffer = block_sweep(
         advance_pair,
         pair_init,
-        (
-            lax.all_gather(keys, "seq", axis=0, tiled=True),
-            lax.all_gather(b_local, "seq", axis=0, tiled=True),
-        ),
+        (mix_sizes(keys, "seq", 0), lax.all_gather(b_local, "seq", axis=0, tiled=True)),
         shard_rows,
     )
     arrived = lax.all_to_all(

time: 207 us -> 251 us (1.21)
  starting transfers between devices: 0.08 us -> 32.3 us
  local copies, waits for them, and re-layouts: 15.1 us -> 26.1 us
  waiting for transfers between devices: 71.4 us -> 77.4 us
  blocking collectives: 64.6 us -> 59.1 us
    ppermute x0 -> x15, starting transfers between devices: none -> 32.3 us  [the longest x7 31.3 us: mix_sizes(): x_next = lax.ppermute(x_next, chip_axis, column)]
    dynamic_update_slice x0 -> x16, local copies, waits for them, and re-layouts: none -> 9.78 us  [the longest x8 4.89 us: mix_sizes(): lax.dynamic_update_slice_in_dim(r_now, clean, (f_now - j) % earlier * w_n...]
    ppermute x0 -> x15, waiting for transfers between devices: none -> 7.03 us  [the longest x8 7 us: mix_sizes(): clean = lax.ppermute(clean, chip_axis, frames)]
    all_gather x1, blocking collectives: 26.4 us -> 21 us  [local(): lax.all_gather(keys, 'seq', axis=0, tiled=True)]
  transfers between devices with their start and end apart: 2 -> 17, of which waited for: 1 -> 8; matrix products, arithmetic and copies ran while one was open for 9% -> 12% of each run, Pallas kernels for 0% -> 0%
where the time goes in v1:
time: 251 us; the launch traced here: 250 us
  waiting for transfers between devices  77.4 us (31%)
  blocking collectives  59.1 us (24%)
  starting transfers between devices  32.3 us (13%)
  local copies, waits for them, and re-layouts  26.1 us (10%)
  matrix products  23.9 us (10%)
  between operations  14.2 us (6%)
  other arithmetic  12.8 us (5%)
  loops' own time  4.22 us (2%)
    reduce_scatter x1, waiting for transfers between devices, local(): lax.psum_scatter(jnp.einsum('td,tn->dn', features, b_grad, preferred_elem...  70.3 us
    ppermute x7, starting transfers between devices, mix_sizes(): x_next = lax.ppermute(x_next, chip_axis, column)  31.3 us
    all_gather x1, blocking collectives, local(): lax.all_gather(keys, 'seq', axis=0, tiled=True)  21 us
    all_gather x1, blocking collectives, local(): lax.all_gather(b_local, 'seq', axis=0, tiled=True)  20.1 us
    all_to_all x1, blocking collectives, local(): lax.all_to_all(db_buffer.reshape(seq_count, shard_rows, state_width).asty...  18 us
    dot_general x4, matrix products, scores_of(): jnp.einsum('qhd,kd->qhk', query_heads, key_block, preferred_element_type=...  9.4 us
    ppermute x8, waiting for transfers between devices, mix_sizes(): clean = lax.ppermute(clean, chip_axis, frames)  7 us
    dynamic_slice x4, local copies, waits for them, and re-layouts, block_sweep(): running, unused = lax.scan(advance, running, (stacked, offsets))  5.28 us
  transfers between devices with their start and end apart: 17, of which 8 were waited for; matrix products, arithmetic and copies ran while one was open for 12% of the time, Pallas kernels for 0%

profile of v1, /device:TPU:0, one launch (start us, length us, event | category | flops | bytes accessed | tf_op | source)
XLA Modules:
  0.0 250.1 jit_solution(5469355861468666370)
XLA Ops:
  7.7 5.1 %collective-permute-start.1 = (bf16[128,128]{1,0:T(8,128)(2,1)}, bf16[128,128]{1,0:T(8,128)(2,1)S(1)}, u32[]{:S(2)}, u32[]{:S(2)}) collective-permute-start(bf16[128,128]{1,0:T(8,128)(2,1)} %param.12), channel_id=1, source_target_pairs={{0,30},{2,0},{4,2},{6,4},{8,6},{10,8},{12,10},{14,12},{16,14},{18,... | collective-permute-start | bytes 98312 | tf_op jit(solution)/shard_map/ppermute | solution.py:132
  13.5 21.0 %all_gather.11 = bf16[2048,128]{1,0:T(8,128)(2,1)S(1)} all-gather(bf16[128,128]{1,0:T(8,128)(2,1)} %param.12), channel_id=1, replica_groups=mesh['seq'=16,'kv'=2] {'seq'}, dimensions={0}, use_global_device_ids=true | all-gather | bytes 557056 | tf_op jit(solution)/shard_map/all_gather | solution.py:107
  34.5 0.7 select_reduce_fusion.3
  35.2 1.0 copy.21
  36.2 0.8 copy.24
  37.0 15.5 %while.30 = (s32[]{:T(128)}, f32[128,4]{0,1:T(4,128)S(1)}, f32[128,4]{0,1:T(4,128)S(1)}, s32[2]{0:T(128)}, s32[16]{0:T(128)S(1)}, /*index=5*/s32[128]{0:T(128)S(...) while((s32[]{:T(128)}, f32[128,4]{0,1:T(4,128)S(1)}, ...), condition=%wide.region_5.6_spmd.clone, body=%wide.region_1.5_spmd.clone.sunk | while | flops 138624512 | bytes 5032648 | solution.py:28
  37.0 1.3 dynamic_slice.62
  38.4 0.6 add_select_fusion.6
  39.1 0.6 fusion.70
  39.9 2.7 %fusion.71 = (f32[128,4]{0,1:T(4,128)S(1)}, f32[1024,128,4]{1,0,2:T(8,128)}) fusion(pred[128,1024]{0,1:T(8,128)(4,1)S(1)} %broadcast_compare_fusion.4, bf16[128,4,128]{2,0,1:T(8,128)(2,1)} %get-tuple-element.599, bf16[2,1024,128]{2,1,0:T(8,128)(2,1)S(1)} %get-tuple-element.598, s32[]{:T(128)} %get-tuple-element.582), kind=kOutput, calls=%fused_computation.4.clone.1 | convolution fusion | flops 135790080 | bytes 2623492 | tf_op jit(solution)/shard_map/while/body/eval_jaxpr/qhd,kd->qhk/dot_general | solution.py:62
  42.6 2.1 select_reduce_fusion.8
  44.8 1.3 dynamic_slice.62
  46.1 0.6 add_select_fusion.6
  46.8 0.6 fusion.70
  47.7 2.7 %fusion.71 = (f32[128,4]{0,1:T(4,128)S(1)}, f32[1024,128,4]{1,0,2:T(8,128)}) fusion(pred[128,1024]{0,1:T(8,128)(4,1)S(1)} %broadcast_compare_fusion.4, bf16[128,4,128]{2,0,1:T(8,128)(2,1)} %get-tuple-element.599, bf16[2,1024,128]{2,1,0:T(8,128)(2,1)S(1)} %get-tuple-element.598, s32[]{:T(128)} %get-tuple-element.582), kind=kOutput, calls=%fused_computation.4.clone.1 | convolution fusion | flops 135790080 | bytes 2623492 | tf_op jit(solution)/shard_map/while/body/eval_jaxpr/qhd,kd->qhk/dot_general | solution.py:62
  50.4 2.1 select_reduce_fusion.8
  52.5 0.9 broadcast_in_dim.138
  54.8 4.1 %collective-permute-start.3 = (bf16[128,128]{1,0:T(8,128)(2,1)S(1)}, bf16[128,128]{1,0:T(8,128)(2,1)S(1)}, u32[]{:S(2)}, u32[]{:S(2)}) collective-permute-start(bf16[128,128]{1,0:T(8,128)(2,1)S(1)} %collective-permute-done.1), channel_id=1, source_target_pairs={{0,30},{2,0},{4,2},{6,4},{8,6},{10,8},{12,10},{14,12},{16,14},{18,... | collective-permute-start | bytes 98312 | tf_op jit(solution)/shard_map/ppermute | solution.py:132
  60.5 4.4 %collective-permute-start.5 = (bf16[128,128]{1,0:T(8,128)(2,1)S(1)}, bf16[128,128]{1,0:T(8,128)(2,1)S(1)}, u32[]{:S(2)}, u32[]{:S(2)}) collective-permute-start(bf16[128,128]{1,0:T(8,128)(2,1)S(1)} %collective-permute-done.3), channel_id=1, source_target_pairs={{0,30},{2,0},{4,2},{6,4},{8,6},{10,8},{12,10},{14,12},{16,14},{18,... | collective-permute-start | bytes 98312 | tf_op jit(solution)/shard_map/ppermute | solution.py:132
  66.5 4.4 %collective-permute-start.7 = (bf16[128,128]{1,0:T(8,128)(2,1)S(1)}, bf16[128,128]{1,0:T(8,128)(2,1)S(1)}, u32[]{:S(2)}, u32[]{:S(2)}) collective-permute-start(bf16[128,128]{1,0:T(8,128)(2,1)S(1)} %collective-permute-done.5), channel_id=1, source_target_pairs={{0,30},{2,0},{4,2},{6,4},{8,6},{10,8},{12,10},{14,12},{16,14},{18,... | collective-permute-start | bytes 98312 | tf_op jit(solution)/shard_map/ppermute | solution.py:132
  72.5 4.4 %collective-permute-start.9 = (bf16[128,128]{1,0:T(8,128)(2,1)S(1)}, bf16[128,128]{1,0:T(8,128)(2,1)S(1)}, u32[]{:S(2)}, u32[]{:S(2)}) collective-permute-start(bf16[128,128]{1,0:T(8,128)(2,1)S(1)} %collective-permute-done.7), channel_id=1, source_target_pairs={{0,30},{2,0},{4,2},{6,4},{8,6},{10,8},{12,10},{14,12},{16,14},{18,... | collective-permute-start | bytes 98312 | tf_op jit(solution)/shard_map/ppermute | solution.py:132
  78.6 4.4 %collective-permute-start.11 = (bf16[128,128]{1,0:T(8,128)(2,1)S(1)}, bf16[128,128]{1,0:T(8,128)(2,1)S(1)}, u32[]{:S(2)}, u32[]{:S(2)}) collective-permute-start(bf16[128,128]{1,0:T(8,128)(2,1)S(1)} %collective-permute-done.9), channel_id=1, source_target_pairs={{0,30},{2,0},{4,2},{6,4},{8,6},{10,8},{12,10},{14,12},{16,14},{18,... | collective-permute-start | bytes 98312 | tf_op jit(solution)/shard_map/ppermute | solution.py:132
  84.6 4.4 %collective-permute-start.13 = (bf16[128,128]{1,0:T(8,128)(2,1)S(1)}, bf16[128,128]{1,0:T(8,128)(2,1)S(1)}, u32[]{:S(2)}, u32[]{:S(2)}) collective-permute-start(bf16[128,128]{1,0:T(8,128)(2,1)S(1)} %collective-permute-done.11), channel_id=1, source_target_pairs={{0,30},{2,0},{4,2},{6,4},{8,6},{10,8},{12,10},{14,12},{16,14},{18,... | collective-permute-start | bytes 98312 | tf_op jit(solution)/shard_map/ppermute | solution.py:132
  91.9 4.8 %collective-permute-done.14 = bf16[128,128]{1,0:T(8,128)(2,1)S(1)} collective-permute-done((bf16[128,128]{1,0:T(8,128)(2,1)S(1)}, bf16[128,128]{1,0:T(8,128)(2,1)S(1)}, u32[]{:S(2)}, u32[]{:S(2)}) %collective-permute-start.14) | collective-permute-done | bytes 32800 | tf_op jit(solution)/shard_map/ppermute | solution.py:127
  97.3 2.3 fusion.41
  99.6 20.1 %all_gather.10 = bf16[2048,128]{1,0:T(8,128)(2,1)} all-gather(bf16[128,128]{1,0:T(8,128)(2,1)S(1)} %fusion.41), channel_id=1, replica_groups=mesh['seq'=16,'kv'=2] {'seq'}, dimensions={0}, use_global_device_ids=true | all-gather | bytes 557056 | tf_op jit(solution)/shard_map/all_gather | solution.py:141
  119.7 0.9 broadcast_in_dim.135
  120.6 26.6 %while.31 = (s32[]{:T(128)}, f32[128,4,128]{2,0,1:T(8,128)}, bf16[2048,128]{1,0:T(8,128)(2,1)}, s32[2]{0:T(128)}, s32[16]{0:T(128)S(1)}, /*index=5*/s32[128]{0:T...) while((s32[]{:T(128)}, f32[128,4,128]{2,0,1:T(8,128)}, ...), condition=%wide.region_8.9_spmd.clone, body=%wide.region_6.8_spmd.clone.sunk | while | flops 541930496 | bytes 10123537 | solution.py:28
  120.6 1.3 dynamic_slice.66
  121.9 0.7 add_select_fusion.7
  122.6 0.7 fusion.82
  123.5 1.4 fusion.81
  124.9 2.0 fusion.83
  129.4 2.7 %dynamic_update_slice.88 = bf16[2048,128]{1,0:T(8,128)(2,1)} dynamic-update-slice(bf16[2048,128]{1,0:T(8,128)(2,1)} %get-tuple-element.619, bf16[1024,128]{1,0:T(8,128)(2,1)S(1)} %convolution_bitcast_fusion.3, s32[]{:T(128)S(6)} %select_n.347, s32[]{:T(128)} %constant.275.clone.1..sunk.1) | dynamic-update-slice | bytes 524292 | tf_op jit(solution)/shard_map/while/body/eval_jaxpr/dynamic_update_slice | solution.py:93
  132.1 2.1 convolution_add_fusion.2
  134.3 1.3 dynamic_slice.66
  135.6 0.7 add_select_fusion.7
  136.4 0.7 fusion.82
  137.3 1.4 fusion.81
  138.7 2.0 fusion.83
  143.1 1.8 dynamic_update_slice.88
  144.9 2.2 convolution_add_fusion.2
  147.2 18.0 %all_to_all.5 = bf16[16,128,128]{2,1,0:T(8,128)(2,1)S(1)} all-to-all(bf16[16,128,128]{2,1,0:T(8,128)(2,1)} %bitcast.109), channel_id=1, replica_groups=mesh['seq'=16,'kv'=2] {'seq'}, dimensions={0} | all-to-all | bytes 1048576 | tf_op jit(solution)/shard_map/all_to_all | solution.py:144
  165.2 4.3 %convolution_bitcast_fusion.1 = f32[8192,128]{0,1:T(8,128)} fusion(bf16[128,128]{1,0:T(8,128)(2,1)S(1)} %reduce_sum.58, bf16[128,8192]{1,0:T(8,128)(2,1)} %all-gather.2.cloned.1.call-done), kind=kOutput, calls=%fused_computation.64 | convolution fusion | flops 268435456 | bytes 6324224 | tf_op jit(solution)/shard_map/td,tn->dn/dot_general | solution.py:153
  169.5 0.9 copy-done.1
  170.4 0.7 copy_bitcast_fusion
  171.1 70.3 %reduce-scatter.2.cloned.1.call-done = f32[512,128]{0,1:T(8,128)} async-done(((f32[8192,128]{0,1:T(8,128)}), f32[512,128]{0,1:T(8,128)}) %reduce-scatter.2.cloned.1.call-update) | async-done | bytes 262160 | tf_op jit(solution)/shard_map/reduce_scatter | solution.py:152
  241.5 1.8 copy.26
  (77 shorter events, 16.1 us)
Async XLA Ops:
  7.2 90.1 %copy-start = (bf16[1,8192,128]{2,1,0:T(8,128)(2,1)S(1)}, bf16[1,8192,128]{2,1,0:T(8,128)(2,1)}, u32[]{:S(2)}) copy-start(bf16[1,8192,128]{2,1,0:T(8,128)(2,1)} %param.15) | copy-start | bytes 6291460
  7.2 29.8 %copy-start.4 = (s32[16]{0:T(128)S(1)}, s32[16]{0:T(128)}, u32[]{:S(2)}) copy-start(s32[16]{0:T(128)} %param.10) | copy-start | bytes 196
  7.2 90.1 %all-gather.2.cloned.1.call-start = ((), (), s32[]{:S(2)}) async-start(), calls=%async_computation.2 | async-start | bytes 3145728 | tf_op jit(solution)/shard_map/all_gather | solution.py:53
  7.2 47.1 %collective-permute-start = (bf16[128,128]{1,0:T(8,128)(2,1)}, bf16[128,128]{1,0:T(8,128)(2,1)S(1)}, u32[]{:S(2)}, u32[]{:S(2)}) collective-permute-start(bf16[128,128]{1,0:T(8,128)(2,1)} %param.12), channel_id=1, source_target_pairs={{0,2},{2,4},{4,6},{6,8},{8,10},{10,12},{12,14},{14,16},{16,18},{18... | collective-permute-start | bytes 98312 | tf_op jit(solution)/shard_map/ppermute | solution.py:127
  7.7 47.0 %collective-permute-start.1 = (bf16[128,128]{1,0:T(8,128)(2,1)}, bf16[128,128]{1,0:T(8,128)(2,1)S(1)}, u32[]{:S(2)}, u32[]{:S(2)}) collective-permute-start(bf16[128,128]{1,0:T(8,128)(2,1)} %param.12), channel_id=1, source_target_pairs={{0,30},{2,0},{4,2},{6,4},{8,6},{10,8},{12,10},{14,12},{16,14},{18,... | collective-permute-start | bytes 98312 | tf_op jit(solution)/shard_map/ppermute | solution.py:132
  12.8 228.6 %reduce-scatter.2.cloned.1.call-start = ((), (), s32[]{:S(2)}) async-start(), calls=%async_computation.3 | async-start | bytes 4456448 | tf_op jit(solution)/shard_map/reduce_scatter | solution.py:152
  37.0 16.4 %copy-start.2 = (bf16[128,128]{1,0:T(8,128)(2,1)S(1)}, bf16[128,128]{1,0:T(8,128)(2,1)}, u32[]{:S(2)}) copy-start(bf16[128,128]{1,0:T(8,128)(2,1)} %param.12) | copy-start | bytes 98308
  37.0 17.0 %copy-start.3 = (bf16[128,512]{1,0:T(8,128)(2,1)S(1)}, bf16[128,512]{1,0:T(8,128)(2,1)}, u32[]{:S(2)}) copy-start(bf16[128,512]{1,0:T(8,128)(2,1)} %param.13) | copy-start | bytes 393220
  54.4 6.1 %collective-permute-start.2 = (bf16[128,128]{1,0:T(8,128)(2,1)S(1)}, bf16[128,128]{1,0:T(8,128)(2,1)S(1)}, u32[]{:S(2)}, u32[]{:S(2)}) collective-permute-start(bf16[128,128]{1,0:T(8,128)(2,1)S(1)} %collective-permute-done), channel_id=1, source_target_pairs={{0,2},{2,4},{4,6},{6,8},{8,10},{10,12},{12,14},{14,16},{16,18},{18... | collective-permute-start | bytes 98312 | tf_op jit(solution)/shard_map/ppermute | solution.py:127
  54.8 5.7 %collective-permute-start.3 = (bf16[128,128]{1,0:T(8,128)(2,1)S(1)}, bf16[128,128]{1,0:T(8,128)(2,1)S(1)}, u32[]{:S(2)}, u32[]{:S(2)}) collective-permute-start(bf16[128,128]{1,0:T(8,128)(2,1)S(1)} %collective-permute-done.1), channel_id=1, source_target_pairs={{0,30},{2,0},{4,2},{6,4},{8,6},{10,8},{12,10},{14,12},{16,14},{18,... | collective-permute-start | bytes 98312 | tf_op jit(solution)/shard_map/ppermute | solution.py:132
  60.5 6.0 %collective-permute-start.4 = (bf16[128,128]{1,0:T(8,128)(2,1)S(1)}, bf16[128,128]{1,0:T(8,128)(2,1)S(1)}, u32[]{:S(2)}, u32[]{:S(2)}) collective-permute-start(bf16[128,128]{1,0:T(8,128)(2,1)S(1)} %collective-permute-done.2), channel_id=1, source_target_pairs={{0,2},{2,4},{4,6},{6,8},{8,10},{10,12},{12,14},{14,16},{16,18},{18... | collective-permute-start | bytes 98312 | tf_op jit(solution)/shard_map/ppermute | solution.py:127
  60.5 6.0 %collective-permute-start.5 = (bf16[128,128]{1,0:T(8,128)(2,1)S(1)}, bf16[128,128]{1,0:T(8,128)(2,1)S(1)}, u32[]{:S(2)}, u32[]{:S(2)}) collective-permute-start(bf16[128,128]{1,0:T(8,128)(2,1)S(1)} %collective-permute-done.3), channel_id=1, source_target_pairs={{0,30},{2,0},{4,2},{6,4},{8,6},{10,8},{12,10},{14,12},{16,14},{18,... | collective-permute-start | bytes 98312 | tf_op jit(solution)/shard_map/ppermute | solution.py:132
  66.5 6.0 %collective-permute-start.6 = (bf16[128,128]{1,0:T(8,128)(2,1)S(1)}, bf16[128,128]{1,0:T(8,128)(2,1)S(1)}, u32[]{:S(2)}, u32[]{:S(2)}) collective-permute-start(bf16[128,128]{1,0:T(8,128)(2,1)S(1)} %collective-permute-done.4), channel_id=1, source_target_pairs={{0,2},{2,4},{4,6},{6,8},{8,10},{10,12},{12,14},{14,16},{16,18},{18... | collective-permute-start | bytes 98312 | tf_op jit(solution)/shard_map/ppermute | solution.py:127
  66.5 6.0 %collective-permute-start.7 = (bf16[128,128]{1,0:T(8,128)(2,1)S(1)}, bf16[128,128]{1,0:T(8,128)(2,1)S(1)}, u32[]{:S(2)}, u32[]{:S(2)}) collective-permute-start(bf16[128,128]{1,0:T(8,128)(2,1)S(1)} %collective-permute-done.5), channel_id=1, source_target_pairs={{0,30},{2,0},{4,2},{6,4},{8,6},{10,8},{12,10},{14,12},{16,14},{18,... | collective-permute-start | bytes 98312 | tf_op jit(solution)/shard_map/ppermute | solution.py:132
  72.5 6.0 %collective-permute-start.8 = (bf16[128,128]{1,0:T(8,128)(2,1)S(1)}, bf16[128,128]{1,0:T(8,128)(2,1)S(1)}, u32[]{:S(2)}, u32[]{:S(2)}) collective-permute-start(bf16[128,128]{1,0:T(8,128)(2,1)S(1)} %collective-permute-done.6), channel_id=1, source_target_pairs={{0,2},{2,4},{4,6},{6,8},{8,10},{10,12},{12,14},{14,16},{16,18},{18... | collective-permute-start | bytes 98312 | tf_op jit(solution)/shard_map/ppermute | solution.py:127
  72.5 6.0 %collective-permute-start.9 = (bf16[128,128]{1,0:T(8,128)(2,1)S(1)}, bf16[128,128]{1,0:T(8,128)(2,1)S(1)}, u32[]{:S(2)}, u32[]{:S(2)}) collective-permute-start(bf16[128,128]{1,0:T(8,128)(2,1)S(1)} %collective-permute-done.7), channel_id=1, source_target_pairs={{0,30},{2,0},{4,2},{6,4},{8,6},{10,8},{12,10},{14,12},{16,14},{18,... | collective-permute-start | bytes 98312 | tf_op jit(solution)/shard_map/ppermute | solution.py:132
  78.6 6.0 %collective-permute-start.10 = (bf16[128,128]{1,0:T(8,128)(2,1)S(1)}, bf16[128,128]{1,0:T(8,128)(2,1)S(1)}, u32[]{:S(2)}, u32[]{:S(2)}) collective-permute-start(bf16[128,128]{1,0:T(8,128)(2,1)S(1)} %collective-permute-done.8), channel_id=1, source_target_pairs={{0,2},{2,4},{4,6},{6,8},{8,10},{10,12},{12,14},{14,16},{16,18},{18... | collective-permute-start | bytes 98312 | tf_op jit(solution)/shard_map/ppermute | solution.py:127
  78.6 6.0 %collective-permute-start.11 = (bf16[128,128]{1,0:T(8,128)(2,1)S(1)}, bf16[128,128]{1,0:T(8,128)(2,1)S(1)}, u32[]{:S(2)}, u32[]{:S(2)}) collective-permute-start(bf16[128,128]{1,0:T(8,128)(2,1)S(1)} %collective-permute-done.9), channel_id=1, source_target_pairs={{0,30},{2,0},{4,2},{6,4},{8,6},{10,8},{12,10},{14,12},{16,14},{18,... | collective-permute-start | bytes 98312 | tf_op jit(solution)/shard_map/ppermute | solution.py:132
  84.6 6.0 %collective-permute-start.12 = (bf16[128,128]{1,0:T(8,128)(2,1)S(1)}, bf16[128,128]{1,0:T(8,128)(2,1)S(1)}, u32[]{:S(2)}, u32[]{:S(2)}) collective-permute-start(bf16[128,128]{1,0:T(8,128)(2,1)S(1)} %collective-permute-done.10), channel_id=1, source_target_pairs={{0,2},{2,4},{4,6},{6,8},{8,10},{10,12},{12,14},{14,16},{16,18},{18... | collective-permute-start | bytes 98312 | tf_op jit(solution)/shard_map/ppermute | solution.py:127
  84.6 6.7 %collective-permute-start.13 = (bf16[128,128]{1,0:T(8,128)(2,1)S(1)}, bf16[128,128]{1,0:T(8,128)(2,1)S(1)}, u32[]{:S(2)}, u32[]{:S(2)}) collective-permute-start(bf16[128,128]{1,0:T(8,128)(2,1)S(1)} %collective-permute-done.11), channel_id=1, source_target_pairs={{0,30},{2,0},{4,2},{6,4},{8,6},{10,8},{12,10},{14,12},{16,14},{18,... | collective-permute-start | bytes 98312 | tf_op jit(solution)/shard_map/ppermute | solution.py:132
  90.6 6.0 %collective-permute-start.14 = (bf16[128,128]{1,0:T(8,128)(2,1)S(1)}, bf16[128,128]{1,0:T(8,128)(2,1)S(1)}, u32[]{:S(2)}, u32[]{:S(2)}) collective-permute-start(bf16[128,128]{1,0:T(8,128)(2,1)S(1)} %collective-permute-done.12), channel_id=1, source_target_pairs={{0,2},{2,4},{4,6},{6,8},{8,10},{10,12},{12,14},{14,16},{16,18},{18... | collective-permute-start | bytes 98312 | tf_op jit(solution)/shard_map/ppermute | solution.py:127
  169.5 0.9 copy-start.1
Sparse Core Ops, SparseCore 0:
  12.9 32.4 all-gather.1
  169.6 71.7 reduce-scatter.1
